TPU v7x, 128 devices: a whole 4x4x4 slice. The times are simulated.
128 devices in a mesh: leaf: 8 (over z, core), sub: 16 (over x, y).
Axes of the slice: x: 4, y: 4, z: 4, core: 2. Of those that a mesh axis runs over, the one named last changes fastest.
Arguments:
- leaf_matrix: float32 [128, 512, 512], P(('leaf', 'sub')), may hold values from 0 to 4, as said below
- leaf_source: float32 [128, 512], P(('leaf', 'sub')), may hold values from -6 to 6
- observe: float32 [128, 512], P(('leaf', 'sub')), may hold values from -6 to 6
- zone_ids: int32 [128, 512], P(('leaf', 'sub')), may hold values from 0 to 16383
- log_perm: float32 [16384], P(('leaf', 'sub')), may hold values from -1 to 1
- block_map: int32 [254, 4], replicated, may hold values from 0 to 6, as said below
Outputs:
- leaf_solution: float32 [128, 512], P(('leaf', 'sub'))
- gradient: float32 [16384], P(('leaf', 'sub'))
Inputs may be any that keep to these rules, and one draw needn't show every extreme that they name: `block_map`: rows 2q and 2q + 1 (sibling nodes) each hold 4 distinct blocks; together they name every value from 0 to 6, sharing exactly one. Each leaf_matrix[d] is symmetric and positive definite.
All inputs are finite; a program needn't handle non-finite values.
Results may differ from a plain program's by a relative error of at most 0.0003.
Values sent between devices are 32-bit elements; how exact they have to be, the bound alone decides.
No kernel may reach another device: no remote copies, remote signals or barrier semaphores. Data moves between devices by JAX's collectives and lax.ppermute only.
A program may use at most 128 MiB of HBM per device.

v0:
```python
import jax
import jax.numpy as jnp
from jax import lax
from jax.sharding import PartitionSpec as P

EXACT_ARITHMETIC = lax.Precision.HIGHEST


def partner_2(block, axis, bit):
    count = lax.axis_size(axis)
    route = []
    for low in range(count):
        high = low | 1 << bit
        if high != low and high < count:
            route += [(low, high), (high, low)]
    return lax.ppermute(block, axis, route)


def lower_triangle_solve(front_factor, rhs, transpose=False):
    return lax.linalg.triangular_solve(
        front_factor, rhs, left_side=True, lower=True, transpose_a=transpose
    )


def selector(block_rows, parent_blocks):
    return (jnp.arange(parent_blocks, dtype=jnp.int32)[:, None] == block_rows[None, :]).astype(
        jnp.float32
    )


def extend_add(matrix, right_vector, block_rows):
    block_count = block_rows.shape[0]
    block_width = matrix.shape[0] // block_count
    parent_blocks = 2 * block_count - 1
    chooser = selector(block_rows, parent_blocks)
    blocked = matrix.reshape(block_count, block_width, block_count, block_width)
    blocked = jnp.einsum("pi,iajb->pajb", chooser, blocked, precision=EXACT_ARITHMETIC)
    blocked = jnp.einsum("pajb,qj->paqb", blocked, chooser, precision=EXACT_ARITHMETIC)
    spread = jnp.einsum(
        "pi,kia->kpa",
        chooser,
        right_vector.reshape(2, block_count, block_width),
        precision=EXACT_ARITHMETIC,
    )
    parent_size = parent_blocks * block_width
    return (blocked.reshape(parent_size, parent_size), spread.reshape(2, parent_size))


def assemble(matrix, right_vector, partner, block_map, device_count, tree_index, level_index):
    node_count = device_count >> level_index
    node_place = tree_index >> level_index
    my_rows = lax.dynamic_index_in_dim(block_map, node_count + node_place - 2, 0, keepdims=False)
    their_rows = lax.dynamic_index_in_dim(
        block_map, node_count + (node_place ^ 1) - 2, 0, keepdims=False
    )
    first_m, first_v = extend_add(matrix, right_vector, my_rows)
    second_m, second_v = extend_add(partner[0], partner[1], their_rows)
    return (first_m + second_m, first_v + second_v, my_rows)


def factor_front(parent_node, parent_vector, frontal_width):
    elimination_count = parent_node.shape[0] - frontal_width
    front_factor = jnp.linalg.cholesky(parent_node[:elimination_count, :elimination_count])
    interface_coupling = lower_triangle_solve(
        front_factor, parent_node[:elimination_count, elimination_count:]
    )
    reduced_system = lower_triangle_solve(front_factor, parent_vector[:, :elimination_count].T)
    updated_vector = (
        parent_vector[:, elimination_count:]
        - jnp.dot(interface_coupling.T, reduced_system, precision=EXACT_ARITHMETIC).T
    )
    return (front_factor, interface_coupling, reduced_system, updated_vector)


def full_schur(parent_node, interface_coupling, frontal_width):
    elimination_count = parent_node.shape[0] - frontal_width
    return parent_node[elimination_count:, elimination_count:] - jnp.dot(
        interface_coupling.T, interface_coupling, precision=EXACT_ARITHMETIC
    )


def recover(front_factor, interface_coupling, reduced_system, kept_part):
    upper_part = lower_triangle_solve(
        front_factor,
        reduced_system - jnp.dot(interface_coupling, kept_part.T, precision=EXACT_ARITHMETIC),
        True,
    )
    return jnp.concatenate([upper_part.T, kept_part], axis=1)


def restrict(solution, block_rows):
    block_count = block_rows.shape[0]
    parent_blocks = 2 * block_count - 1
    block_width = solution.shape[1] // parent_blocks
    chooser = selector(block_rows, parent_blocks)
    picked = jnp.einsum(
        "pi,kpa->kia",
        chooser,
        solution.reshape(2, parent_blocks, block_width),
        precision=EXACT_ARITHMETIC,
    )
    return picked.reshape(2, block_count * block_width)


def shards(leaf_matrix, leaf_source, observe, zone_ids, log_perm, block_map):
    leaf_count = lax.axis_size("leaf")
    sub_count = lax.axis_size("sub")
    device_count = leaf_count * sub_count
    leaf_place = lax.axis_index("leaf")
    sub_place = lax.axis_index("sub")
    tree_index = leaf_place + leaf_count * sub_place
    frontal_width = leaf_matrix.shape[-1]
    all_zones = lax.all_gather(log_perm, ("leaf", "sub"), axis=0, tiled=True)
    cell_zones = zone_ids[0]
    perm_diag = jnp.exp(all_zones[cell_zones])
    matrix = leaf_matrix[0] + jnp.eye(frontal_width, dtype=jnp.float32) * perm_diag[None, :]
    right_vector = jnp.stack([leaf_source[0], observe[0]])
    stored = []
    leaf_bits = leaf_count.bit_length() - 1
    sub_bits = sub_count.bit_length() - 1
    for bit_index in range(leaf_bits):
        partner = partner_2((matrix, right_vector), "leaf", bit_index)
        parent_node, parent_vector, my_rows = assemble(
            matrix, right_vector, partner, block_map, device_count, tree_index, bit_index
        )
        front_factor, interface_coupling, reduced_system, updated_vector = factor_front(
            parent_node, parent_vector, frontal_width
        )
        matrix = full_schur(parent_node, interface_coupling, frontal_width)
        right_vector = updated_vector
        stored.append((front_factor, interface_coupling, reduced_system, my_rows))
    for bit_index in range(sub_bits):
        partner = partner_2((matrix, right_vector), "sub", bit_index)
        parent_node, parent_vector, my_rows = assemble(
            matrix,
            right_vector,
            partner,
            block_map,
            device_count,
            tree_index,
            leaf_bits + bit_index,
        )
        front_factor, interface_coupling, reduced_system, updated_vector = factor_front(
            parent_node, parent_vector, frontal_width
        )
        matrix = full_schur(parent_node, interface_coupling, frontal_width)
        right_vector = updated_vector
        stored.append((front_factor, interface_coupling, reduced_system, my_rows))
    root_factor = jnp.linalg.cholesky(matrix)
    middle = lower_triangle_solve(root_factor, right_vector.T)
    solution = lower_triangle_solve(root_factor, middle, True).T
    for front_factor, interface_coupling, reduced_system, my_rows in reversed(stored):
        solution = restrict(
            recover(front_factor, interface_coupling, reduced_system, solution), my_rows
        )
    terms = -perm_diag * solution[0] * solution[1]
    partial_sum = jax.ops.segment_sum(terms, cell_zones, num_segments=all_zones.shape[0])
    gradient = lax.psum_scatter(partial_sum, ("leaf", "sub"), scatter_dimension=0, tiled=True)
    return (solution[0][None, :], gradient)


def solution(mesh):
    in_specs = (
        P(("leaf", "sub"), None, None),
        P(("leaf", "sub"), None),
        P(("leaf", "sub"), None),
        P(("leaf", "sub"), None),
        P(("leaf", "sub")),
        P(),
    )
    out_specs = (P(("leaf", "sub"), None), P(("leaf", "sub")))
    return jax.shard_map(shards, mesh=mesh, in_specs=in_specs, out_specs=out_specs, check_vma=False)
```

profile of v0, /device:TPU:1, one launch (start us, length us, event | category | flops | bytes accessed | tf_op | source)
XLA Modules:
  0.0 1570.4 jit_solution(13316607199414666465)
XLA Ops:
  7.2 51.6 %all-gather = f32[128,1,128]{2,1,0:T(1,128)S(1)} all-gather(f32[1,1,128]{2,1,0:T(1,128)} %bitcast.954), channel_id=1, replica_groups=mesh['leaf'=8,'sub'=16] {'leaf','sub'}, dimensions={0}, use_global_device_ids=true | all-gather | bytes 66048 | tf_op jit(solution)/shard_map/all_gather | solution.py:113
  89.4 11.9 cholesky.666
  115.0 11.7 cholesky.678
  139.5 11.7 cholesky.693
  166.0 30.1 %custom-call.127 = f32[3,128,128]{1,2,0:T(8,128)} custom-call(f32[3,128,128]{2,1,0:T(8,128)S(1)} %get-tuple-element.168), custom_call_target="InvertDiagBlocksLowerTriangular" | custom-call | tf_op jit(solution)/shard_map/triangular_solve/custom-call.14 | solution.py:20
  246.6 12.7 cholesky.708
  261.3 10.6 custom-call.95
  276.3 12.5 cholesky.720
  290.0 10.6 custom-call.96
  304.2 12.7 cholesky.735
  335.7 30.9 %custom-call.126 = f32[3,128,128]{1,2,0:T(8,128)} custom-call(f32[3,128,128]{2,1,0:T(8,128)} %get-tuple-element.167), custom_call_target="InvertDiagBlocksLowerTriangular" | custom-call | tf_op jit(solution)/shard_map/triangular_solve/custom-call.14 | solution.py:20
  417.8 12.7 cholesky.750
  432.5 10.6 custom-call.99
  447.5 12.5 cholesky.762
  461.2 10.6 custom-call.100
  475.5 12.7 cholesky.777
  506.4 30.9 %custom-call.125 = f32[3,128,128]{1,2,0:T(8,128)} custom-call(f32[3,128,128]{2,1,0:T(8,128)} %get-tuple-element.166), custom_call_target="InvertDiagBlocksLowerTriangular" | custom-call | tf_op jit(solution)/shard_map/triangular_solve/custom-call.14 | solution.py:20
  586.1 12.7 cholesky.792
  600.9 10.6 custom-call.103
  615.8 12.5 cholesky.804
  629.6 10.6 custom-call.104
  643.8 12.7 cholesky.819
  675.1 30.9 %custom-call.124 = f32[3,128,128]{1,2,0:T(8,128)} custom-call(f32[3,128,128]{2,1,0:T(8,128)} %get-tuple-element.165), custom_call_target="InvertDiagBlocksLowerTriangular" | custom-call | tf_op jit(solution)/shard_map/triangular_solve/custom-call.14 | solution.py:20
  755.4 12.7 cholesky.834
  770.2 10.6 custom-call.107
  785.1 12.5 cholesky.846
  798.9 10.6 custom-call.108
  813.1 12.7 cholesky.861
  834.5 10.7 while.46
  845.2 30.9 %custom-call.123 = f32[3,128,128]{1,2,0:T(8,128)} custom-call(f32[3,128,128]{2,1,0:T(8,128)} %get-tuple-element.164), custom_call_target="InvertDiagBlocksLowerTriangular" | custom-call | tf_op jit(solution)/shard_map/triangular_solve/custom-call.14 | solution.py:20
  923.2 12.7 cholesky.876
  938.0 10.6 custom-call.111
  953.0 12.5 cholesky.888
  981.1 12.7 cholesky.903
  1002.5 10.8 while.45
  1013.3 30.9 %custom-call.122 = f32[3,128,128]{1,2,0:T(8,128)} custom-call(f32[3,128,128]{2,1,0:T(8,128)} %get-tuple-element.163), custom_call_target="InvertDiagBlocksLowerTriangular" | custom-call | tf_op jit(solution)/shard_map/triangular_solve/custom-call.14 | solution.py:20
  1095.5 12.7 cholesky.918
  1110.2 10.6 custom-call.115
  1125.2 12.5 cholesky.930
  1138.9 10.6 custom-call.116
  1153.2 12.9 cholesky.945
  1184.6 30.9 %custom-call.121 = f32[3,128,128]{1,2,0:T(8,128)} custom-call(f32[3,128,128]{2,1,0:T(8,128)} %get-tuple-element.162), custom_call_target="InvertDiagBlocksLowerTriangular" | custom-call | tf_op jit(solution)/shard_map/triangular_solve/custom-call.14 | solution.py:20
  1225.4 11.7 cholesky.198
  1249.8 11.9 cholesky.221
  1273.1 11.7 cholesky.315
  1296.1 11.9 cholesky.328
  1323.8 40.1 %custom-call.44 = f32[4,128,128]{1,2,0:T(8,128)S(1)} custom-call(f32[4,128,128]{2,1,0:T(8,128)} %get-tuple-element.39), custom_call_target="InvertDiagBlocksLowerTriangular" | custom-call | tf_op jit(solution)/shard_map/triangular_solve | solution.py:20
  1417.1 144.8 %all-reduce.5.cloned.1.call-done = f32[16384]{0:T(1024)} async-done(((f32[16384]{0:T(1024)}), f32[16384]{0:T(1024)}) %all-reduce.5.cloned.1.call-update) | async-done | bytes 65552
  (775 shorter events, 717.5 us)
Async XLA Ops:
  7.2 59.3 %copy-start = (f32[1,512,512]{2,1,0:T(8,128)S(1)}, f32[1,512,512]{2,1,0:T(8,128)}, u32[]{:S(2)}) copy-start(f32[1,512,512]{2,1,0:T(8,128)} %param.17) | copy-start | bytes 3145732
  7.2 59.2 %copy-start.100 = (f32[1,512]{1,0:T(1,128)S(1)}, f32[1,512]{1,0:T(1,128)}, u32[]{:S(2)}) copy-start(f32[1,512]{1,0:T(1,128)} %param.19) | copy-start | bytes 6148
  7.2 59.2 %copy-start.101 = (f32[1,512]{1,0:T(1,128)S(1)}, f32[1,512]{1,0:T(1,128)}, u32[]{:S(2)}) copy-start(f32[1,512]{1,0:T(1,128)} %param.18) | copy-start | bytes 6148
  7.2 1554.7 %all-reduce.5.cloned.1.call-start = ((), (), s32[]{:S(2)}) async-start(), calls=%async_computation | async-start | bytes 131072
  65.1 10.3 collective-permute-start
  66.4 8.7 collective-permute-start.1
  68.0 154.7 %copy-start.71 = (s32[4]{0:T(128)}, s32[4]{0:T(128)S(1)}, u32[]{:S(2)}) copy-start(s32[4]{0:T(128)S(1)} %get-tuple-element.179) | copy-start | bytes 52
  207.7 25.5 %collective-permute-start.2 = (f32[512,512]{1,0:T(8,128)}, f32[512,512]{1,0:T(8,128)S(1)}, u32[]{:S(2)}, u32[]{:S(2)}) collective-permute-start(f32[512,512]{1,0:T(8,128)} %convolution_subtract_fusion.6), channel_id=1, source_target_pairs={{0,32},{32,0},{16,48},{48,16},{64,96},{96,64},{80,112},{112,80},{1... | collective-permute-start | bytes 3145736 | tf_op jit(solution)/shard_map/ppermute | solution.py:16
  214.5 17.8 %collective-permute-start.3 = (f32[2,512]{1,0:T(2,128)S(1)}, f32[2,512]{1,0:T(2,128)S(1)}, u32[]{:S(2)}, u32[]{:S(2)}) collective-permute-start(f32[2,512]{1,0:T(2,128)S(1)} %slice_subtract_fusion.6), channel_id=1, source_target_pairs={{0,32},{32,0},{16,48},{48,16},{64,96},{96,64},{80,112},{112,80},{1... | collective-permute-start | bytes 12296 | tf_op jit(solution)/shard_map/ppermute | solution.py:16
  378.4 26.1 %collective-permute-start.4 = (f32[512,512]{1,0:T(8,128)}, f32[512,512]{1,0:T(8,128)S(1)}, u32[]{:S(2)}, u32[]{:S(2)}) collective-permute-start(f32[512,512]{1,0:T(8,128)} %convolution_subtract_fusion.5), channel_id=1, source_target_pairs={{0,64},{64,0},{16,80},{80,16},{32,96},{96,32},{48,112},{112,48},{1... | collective-permute-start | bytes 3145736 | tf_op jit(solution)/shard_map/ppermute | solution.py:16
  387.4 16.1 %collective-permute-start.5 = (f32[2,512]{1,0:T(2,128)S(1)}, f32[2,512]{1,0:T(2,128)S(1)}, u32[]{:S(2)}, u32[]{:S(2)}) collective-permute-start(f32[2,512]{1,0:T(2,128)S(1)} %slice_subtract_fusion.5), channel_id=1, source_target_pairs={{0,64},{64,0},{16,80},{80,16},{32,96},{96,32},{48,112},{112,48},{1... | collective-permute-start | bytes 12296 | tf_op jit(solution)/shard_map/ppermute | solution.py:16
  549.0 23.7 %collective-permute-start.6 = (f32[512,512]{1,0:T(8,128)}, f32[512,512]{1,0:T(8,128)S(1)}, u32[]{:S(2)}, u32[]{:S(2)}) collective-permute-start(f32[512,512]{1,0:T(8,128)} %convolution_subtract_fusion.4), channel_id=1, source_target_pairs={{0,1},{1,0},{2,3},{3,2},{4,5},{5,4},{6,7},{7,6},{8,9},{9,8},{10,11... | collective-permute-start | bytes 3145736 | tf_op jit(solution)/shard_map/ppermute | solution.py:16
  557.2 14.6 collective-permute-start.7
  717.7 24.3 %collective-permute-start.8 = (f32[512,512]{1,0:T(8,128)}, f32[512,512]{1,0:T(8,128)S(1)}, u32[]{:S(2)}, u32[]{:S(2)}) collective-permute-start(f32[512,512]{1,0:T(8,128)} %convolution_subtract_fusion.3), channel_id=1, source_target_pairs={{0,2},{2,0},{1,3},{3,1},{4,6},{6,4},{5,7},{7,5},{8,10},{10,8},{9,1... | collective-permute-start | bytes 3145736 | tf_op jit(solution)/shard_map/ppermute | solution.py:16
  727.3 13.8 collective-permute-start.9
  887.9 21.8 %collective-permute-start.10 = (f32[512,512]{1,0:T(8,128)}, f32[512,512]{1,0:T(8,128)S(1)}, u32[]{:S(2)}, u32[]{:S(2)}) collective-permute-start(f32[512,512]{1,0:T(8,128)} %convolution_subtract_fusion.2), channel_id=1, source_target_pairs={{0,4},{4,0},{1,5},{5,1},{2,6},{6,2},{3,7},{7,3},{8,12},{12,8},{9,1... | collective-permute-start | bytes 3145736 | tf_op jit(solution)/shard_map/ppermute | solution.py:16
  896.3 12.5 collective-permute-start.11
  1056.0 22.4 %collective-permute-start.12 = (f32[512,512]{1,0:T(8,128)}, f32[512,512]{1,0:T(8,128)S(1)}, u32[]{:S(2)}, u32[]{:S(2)}) collective-permute-start(f32[512,512]{1,0:T(8,128)} %convolution_subtract_fusion.1), channel_id=1, source_target_pairs={{0,8},{8,0},{1,9},{9,1},{2,10},{10,2},{3,11},{11,3},{4,12},{12,4},... | collective-permute-start | bytes 3145736 | tf_op jit(solution)/shard_map/ppermute | solution.py:16
  1066.3 11.3 collective-permute-start.13
  1237.2 76.2 %copy-start.112 = (s32[4]{0:T(128)S(1)}, s32[4]{0:T(128)}, u32[]{:S(2)}) copy-start(s32[4]{0:T(128)} %iota_multiply_fusion.1) | copy-start | bytes 52
  1247.1 116.8 %copy-start.51 = (f32[384,2]{0,1:T(2,128)S(1)}, f32[384,2]{0,1:T(2,128)}, u32[]{:S(2)}) copy-start(f32[384,2]{0,1:T(2,128)} %slice_bitcast_fusion.96) | copy-start | bytes 9220
  1247.1 117.8 %copy-start.14 = (f32[384,384]{1,0:T(8,128)S(1)}, f32[384,384]{1,0:T(8,128)}, u32[]{:S(2)}) copy-start(f32[384,384]{1,0:T(8,128)} %get-tuple-element.708) | copy-start | bytes 1769476
  1248.5 119.0 %copy-start.13 = (f32[128,512]{1,0:T(8,128)S(1)}, f32[128,512]{1,0:T(8,128)}, u32[]{:S(2)}) copy-start(f32[128,512]{1,0:T(8,128)} %copy-done.12) | copy-start | bytes 786436
  1313.2 64.4 %copy-start.82 = (s32[4]{0:T(128)S(1)}, s32[4]{0:T(128)}, u32[]{:S(2)}) copy-start(s32[4]{0:T(128)} %get-tuple-element.182) | copy-start | bytes 52
  1313.2 64.6 %copy-start.11 = (f32[128,512]{1,0:T(8,128)S(1)}, f32[128,512]{1,0:T(8,128)}, u32[]{:S(2)}) copy-start(f32[128,512]{1,0:T(8,128)} %copy-done.10) | copy-start | bytes 786436
  1313.2 64.6 %copy-start.68 = (f32[128,2]{0,1:T(2,128)S(1)}, f32[128,2]{0,1:T(2,128)}, u32[]{:S(2)}) copy-start(f32[128,2]{0,1:T(2,128)} %copy-done.67) | copy-start | bytes 3076
  1313.2 64.6 %copy-start.99 = (f32[128,2]{0,1:T(2,128)S(1)}, f32[128,2]{0,1:T(2,128)}, u32[]{:S(2)}) copy-start(f32[128,2]{0,1:T(2,128)} %copy-done.98) | copy-start | bytes 3076
  1313.4 71.7 %copy-start.80 = (s32[4]{0:T(128)S(1)}, s32[4]{0:T(128)}, u32[]{:S(2)}) copy-start(s32[4]{0:T(128)} %get-tuple-element.171) | copy-start | bytes 52
  1313.4 71.9 %copy-start.9 = (f32[128,512]{1,0:T(8,128)S(1)}, f32[128,512]{1,0:T(8,128)}, u32[]{:S(2)}) copy-start(f32[128,512]{1,0:T(8,128)} %copy-done.8) | copy-start | bytes 786436
  1313.4 71.9 %copy-start.66 = (f32[128,2]{0,1:T(2,128)S(1)}, f32[128,2]{0,1:T(2,128)}, u32[]{:S(2)}) copy-start(f32[128,2]{0,1:T(2,128)} %copy-done.65) | copy-start | bytes 3076
  1313.4 71.9 %copy-start.97 = (f32[128,2]{0,1:T(2,128)S(1)}, f32[128,2]{0,1:T(2,128)}, u32[]{:S(2)}) copy-start(f32[128,2]{0,1:T(2,128)} %copy-done.96) | copy-start | bytes 3076
  1370.9 28.9 %copy-start.76 = (s32[4]{0:T(128)S(1)}, s32[4]{0:T(128)}, u32[]{:S(2)}) copy-start(s32[4]{0:T(128)} %get-tuple-element.175) | copy-start | bytes 52
  1371.1 29.0 %copy-start.5 = (f32[128,512]{1,0:T(8,128)S(1)}, f32[128,512]{1,0:T(8,128)}, u32[]{:S(2)}) copy-start(f32[128,512]{1,0:T(8,128)} %copy-done.4) | copy-start | bytes 786436
  1371.1 29.0 %copy-start.62 = (f32[128,2]{0,1:T(2,128)S(1)}, f32[128,2]{0,1:T(2,128)}, u32[]{:S(2)}) copy-start(f32[128,2]{0,1:T(2,128)} %copy-done.61) | copy-start | bytes 3076
  1371.1 29.0 %copy-start.93 = (f32[128,2]{0,1:T(2,128)S(1)}, f32[128,2]{0,1:T(2,128)}, u32[]{:S(2)}) copy-start(f32[128,2]{0,1:T(2,128)} %copy-done.92) | copy-start | bytes 3076
  1372.0 29.9 %copy-start.27 = (f32[3,128,128]{1,2,0:T(8,128)S(1)}, f32[3,128,128]{1,2,0:T(8,128)}, u32[]{:S(2)}) copy-start(f32[3,128,128]{1,2,0:T(8,128)} %custom-call.125) | copy-start | bytes 589828
  1373.8 30.9 %copy-start.74 = (s32[4]{0:T(128)S(1)}, s32[4]{0:T(128)}, u32[]{:S(2)}) copy-start(s32[4]{0:T(128)} %get-tuple-element.177) | copy-start | bytes 52
  1373.8 31.1 %copy-start.3 = (f32[128,512]{1,0:T(8,128)S(1)}, f32[128,512]{1,0:T(8,128)}, u32[]{:S(2)}) copy-start(f32[128,512]{1,0:T(8,128)} %copy-done.2) | copy-start | bytes 786436
  1373.9 31.0 %copy-start.19 = (f32[128,512]{1,0:T(8,128)S(1)}, f32[128,512]{1,0:T(8,128)}, u32[]{:S(2)}) copy-start(f32[128,512]{1,0:T(8,128)} %copy-done.18) | copy-start | bytes 786436
  1373.9 31.0 %copy-start.38 = (f32[128,512]{1,0:T(8,128)S(1)}, f32[128,512]{1,0:T(8,128)}, u32[]{:S(2)}) copy-start(f32[128,512]{1,0:T(8,128)} %copy-done.37) | copy-start | bytes 786436
  1373.9 31.0 %copy-start.60 = (f32[128,2]{0,1:T(2,128)S(1)}, f32[128,2]{0,1:T(2,128)}, u32[]{:S(2)}) copy-start(f32[128,2]{0,1:T(2,128)} %copy-done.59) | copy-start | bytes 3076
  1373.9 31.0 %copy-start.91 = (f32[128,2]{0,1:T(2,128)S(1)}, f32[128,2]{0,1:T(2,128)}, u32[]{:S(2)}) copy-start(f32[128,2]{0,1:T(2,128)} %copy-done.90) | copy-start | bytes 3076
  1373.9 31.0 %copy-start.105 = (f32[128,2]{0,1:T(2,128)S(1)}, f32[128,2]{0,1:T(2,128)}, u32[]{:S(2)}) copy-start(f32[128,2]{0,1:T(2,128)} %copy-done.104) | copy-start | bytes 3076
  1379.7 29.1 %copy-start.17 = (f32[128,512]{1,0:T(8,128)S(1)}, f32[128,512]{1,0:T(8,128)}, u32[]{:S(2)}) copy-start(f32[128,512]{1,0:T(8,128)} %copy-done.16) | copy-start | bytes 786436
  1379.7 29.1 %copy-start.36 = (f32[128,512]{1,0:T(8,128)S(1)}, f32[128,512]{1,0:T(8,128)}, u32[]{:S(2)}) copy-start(f32[128,512]{1,0:T(8,128)} %copy-done.35) | copy-start | bytes 786436
  1379.7 29.1 %copy-start.58 = (f32[128,2]{0,1:T(2,128)S(1)}, f32[128,2]{0,1:T(2,128)}, u32[]{:S(2)}) copy-start(f32[128,2]{0,1:T(2,128)} %copy-done.57) | copy-start | bytes 3076
  1379.7 29.1 %copy-start.89 = (f32[128,2]{0,1:T(2,128)S(1)}, f32[128,2]{0,1:T(2,128)}, u32[]{:S(2)}) copy-start(f32[128,2]{0,1:T(2,128)} %copy-done.88) | copy-start | bytes 3076
  1379.7 29.1 %copy-start.103 = (f32[128,2]{0,1:T(2,128)S(1)}, f32[128,2]{0,1:T(2,128)}, u32[]{:S(2)}) copy-start(f32[128,2]{0,1:T(2,128)} %copy-done.102) | copy-start | bytes 3076
  (80 other events, 668.6 us)
Sparse Core Ops, SparseCore 0:
  1416.7 145.2 all-reduce.4
where the time goes:
time: 1590 us; the launch traced here: 1570 us
  other arithmetic  816 us (51%)
  matrix products  296 us (19%)
  waiting for transfers between devices  184 us (12%)
  local copies, waits for them, and re-layouts  172 us (11%)
  blocking collectives  51.6 us (3%)
  between operations  32.8 us (2%)
  starting transfers between devices  18 us (1%)
    another operation x76, other arithmetic, factor_front(): jnp.linalg.cholesky(parent_node[:elimination_count, :elimination_count])  451 us
    another operation x18, other arithmetic, lower_triangle_solve(): lax.linalg.triangular_solve(front_factor, rhs, left_side=True, lower=True...  270 us
    unnamed x2, waiting for transfers between devices  145 us
    another operation x119, matrix products, lower_triangle_solve(): lax.linalg.triangular_solve(front_factor, rhs, left_side=True, lower=True...  110 us
    another operation x15, other arithmetic, shards(): root_factor = jnp.linalg.cholesky(matrix)  79.4 us
    another operation x72, local copies, waits for them, and re-layouts, lower_triangle_solve(): lax.linalg.triangular_solve(front_factor, rhs, left_side=True, lower=True...  75.2 us
    dot_general x14, matrix products, extend_add(): jnp.einsum('pajb,qj->paqb', blocked, chooser, precision=EXACT_ARITHMETIC)  63.2 us
    all_gather x1, blocking collectives, shards(): all_zones = lax.all_gather(log_perm, ('leaf', 'sub'), axis=0, tiled=True)  51.6 us
  transfers between devices with their start and end apart: 15, of which 7 were waited for; matrix products, arithmetic and copies ran while one was open for 6% of the time, Pallas kernels for 0%

commit v1 on v0

v1 whole, which is shorter than its diff:
```python
import functools

import jax
import jax.numpy as jnp
from jax import lax
from jax.experimental import pallas as pl
from jax.experimental.pallas import tpu as pltpu
from jax.sharding import PartitionSpec as P

BW = 128
NB = 4
KEEP = NB - 1
FW = NB * BW
RHS = FW
SHARED = RHS + 8
ROWS = SHARED + BW
COLS = FW + BW
PAIRS = [(i, j) for i in range(NB) for j in range(i, NB)]
PACK = len(PAIRS) * BW + NB * 8
VMEM_LIMIT = 48 * 1024 * 1024


def split(x):
    high = x.astype(jnp.bfloat16)
    return high, (x - high.astype(jnp.float32)).astype(jnp.bfloat16)


def dot_split(a, b):
    one = functools.partial(jnp.dot, preferred_element_type=jnp.float32)
    return one(a[0], b[0]) + (one(a[0], b[1]) + one(a[1], b[0]))


def lanes(x, c):
    return jnp.broadcast_to(x[:, c : c + 1], (8, BW))


def rows(x, j):
    return jnp.broadcast_to(x[j : j + 1, :], (8, BW))


def invert(slabs):
    lane = lax.broadcasted_iota(jnp.int32, (8, BW), 1)
    sub = lax.broadcasted_iota(jnp.int32, (8, BW), 0)
    slabs = list(slabs)
    count = len(slabs)
    for k in range(count):
        cols = [lanes(slabs[k], 8 * k + j) for j in range(8)]
        inside = (lane >= 8 * k) & (lane < 8 * k + 8)
        row = jnp.where(lane == sub + 8 * k, 1.0, jnp.where(inside, 0.0, slabs[k]))
        for j in range(8):
            inv = 1.0 / rows(cols[j], j)
            w = rows(row, j) * inv
            row = jnp.where(sub == j, w, row - cols[j] * w)
            for m in range(j + 1, 8):
                cm = rows(cols[m], j) * inv
                cols[m] = jnp.where(sub == j, cm, cols[m] - cols[j] * cm)
        w = [rows(row, j) for j in range(8)]
        for r in list(range(k + 1, count)) + list(range(k)):
            t0 = jnp.where(inside, 0.0, slabs[r]) - lanes(slabs[r], 8 * k) * w[0]
            t1 = lanes(slabs[r], 8 * k + 1) * w[1]
            for j in range(2, 8, 2):
                t0 = t0 - lanes(slabs[r], 8 * k + j) * w[j]
                t1 = t1 + lanes(slabs[r], 8 * k + j + 1) * w[j + 1]
            slabs[r] = t0 - t1
        slabs[k] = row
    return slabs


def row_of(block):
    return jnp.where(block == NB, SHARED, block * BW)


def sweep(front, inverse, wide, block):
    ro = pl.multiple_of(row_of(block), 8)
    co = pl.multiple_of(block * BW, BW)
    out = invert([front[pl.ds(ro + 8 * r, 8), pl.ds(co, BW)] for r in range(BW // 8)])
    for r in range(BW // 8):
        inverse[8 * r : 8 * r + 8, :] = out[r]
    wide[...] = dot_split(split(inverse[...]), split(front[pl.ds(ro, BW), :]))
    wide[:, pl.ds(co, BW)] = inverse[...]
    w = split(wide[...])
    for at, size in [(i * BW, BW) for i in range(NB)] + [(RHS, 8)]:
        g = split(front[at : at + size, pl.ds(co, BW)])
        front[at : at + size, pl.ds(co, BW)] = jnp.zeros((size, BW), jnp.float32)
        front[at : at + size, :] -= dot_split(g, w)


def place(map_ref, row, other):
    mine = [map_ref[row * NB + i] for i in range(NB)]
    theirs = [map_ref[other * NB + i] for i in range(NB)]
    out = []
    for m in mine:
        both = functools.reduce(jnp.logical_or, [m == t for t in theirs])
        out.append(jnp.where(m >= KEEP, m - KEEP, jnp.where(both, NB, -1)))
    return out


def map_rows(tree, level, devices):
    nodes = devices >> level
    node = tree >> level
    return nodes + node - 2, nodes + (node ^ 1) - 2


def eliminate(front, inverse, wide, flags, blocks, pack):
    def step(n, carry):
        @pl.when(flags[n] == 1)
        def _():
            sweep(front, inverse, wide, lax.rem(n + NB, NB + 1))

        return carry

    lax.fori_loop(1 if blocks == NB else 0, NB + 1, step, 0)
    if pack is not None:
        for p, (i, j) in enumerate(PAIRS):
            pack[p * BW : p * BW + BW, :] = front[i * BW : i * BW + BW, j * BW : j * BW + BW]
        for i in range(NB):
            at = len(PAIRS) * BW + 8 * i
            pack[at : at + 8, :] = front[RHS : RHS + 8, i * BW : i * BW + BW]


def set_flags(flags, map_ref, tree, level, devices):
    if devices >> level == 1:
        for i in range(NB):
            flags[1 + i] = 1
        return
    for i, slot in enumerate(place(map_ref, *map_rows(tree, level, devices))):
        flags[1 + i] = jnp.where(slot < 0, 1, 0)


def leaf_kernel(devices, tree_ref, map_ref, leaf, source, observe, perm, front, pack, inverse, wide, flags):
    front[0:FW, :] = leaf[...]
    eye = lax.broadcasted_iota(jnp.int32, (BW, BW), 0) == lax.broadcasted_iota(jnp.int32, (BW, BW), 1)
    for i in range(NB):
        at = slice(i * BW, i * BW + BW)
        front[at, at] += jnp.where(eye, jnp.broadcast_to(perm[:, at], (BW, BW)), 0.0)
    which = lax.broadcasted_iota(jnp.int32, (8, FW), 0)
    front[RHS : RHS + 8, :] = jnp.where(
        which == 0,
        jnp.broadcast_to(source[...], (8, FW)),
        jnp.where(which == 1, jnp.broadcast_to(observe[...], (8, FW)), 0.0),
    )
    set_flags(flags, map_ref, tree_ref[0], 0, devices)
    eliminate(front, inverse, wide, flags, NB, pack)


def merge_kernel(devices, level, tree_ref, map_ref, own, theirs, front, *rest):
    pack = rest[0] if len(rest) == 5 else None
    inverse, wide, flags, slots = rest[-4:]
    tree = tree_ref[0]
    row, other = map_rows(tree, level, devices)
    mine, yours = place(map_ref, row, other), place(map_ref, other, row)
    flags[0] = functools.reduce(jnp.maximum, [jnp.where(s == NB, 1, 0) for s in mine])
    set_flags(flags, map_ref, tree, level + 1, devices)
    for i in range(NB):
        slots[i] = mine[i]
    front[...] = jnp.zeros(front.shape, jnp.float32)

    def one(p, carry):
        i, j = p // NB, lax.rem(p, NB)
        a, b = slots[i], slots[j]

        @pl.when((a >= 0) & (b >= 0))
        def _():
            front[pl.ds(pl.multiple_of(row_of(a), 8), BW), pl.ds(pl.multiple_of(b * BW, BW), BW)] = own[
                pl.ds(pl.multiple_of(i * BW, BW), BW), pl.ds(pl.multiple_of(j * BW, BW), BW)
            ]

        return carry

    lax.fori_loop(0, NB * NB, one, 0)
    for i in range(NB):

        @pl.when(mine[i] >= 0)
        def _():
            co = pl.ds(pl.multiple_of(mine[i] * BW, BW), BW)
            front[RHS : RHS + 8, co] = own[RHS : RHS + 8, i * BW : i * BW + BW]

    for p, (i, j) in enumerate(PAIRS):
        a, b = yours[i], yours[j]

        @pl.when((a >= 0) & (b >= 0))
        def _():
            block = theirs[p * BW : p * BW + BW, :]
            front[pl.ds(pl.multiple_of(row_of(a), 8), BW), pl.ds(pl.multiple_of(b * BW, BW), BW)] += block
            if i != j:
                front[pl.ds(pl.multiple_of(row_of(b), 8), BW), pl.ds(pl.multiple_of(a * BW, BW), BW)] += block.T

    for i in range(NB):

        @pl.when(yours[i] >= 0)
        def _():
            at = len(PAIRS) * BW + 8 * i
            front[RHS : RHS + 8, pl.ds(pl.multiple_of(yours[i] * BW, BW), BW)] += theirs[at : at + 8, :]

    eliminate(front, inverse, wide, flags, NB + 1, pack)


def recover_kernel(devices, levels, tree_ref, map_ref, *refs):
    fronts, out, kept, solved = refs[: levels + 1], refs[levels + 1], refs[levels + 2], refs[levels + 3]
    tree = tree_ref[0]
    solved[...] = -fronts[levels][RHS : RHS + 8, :]
    for level in reversed(range(levels)):
        front = fronts[level]
        slots = place(map_ref, *map_rows(tree, level, devices))
        for i in range(NB):
            at = slice(i * BW, i * BW + BW)
            kept[:, at] = jnp.zeros((8, BW), jnp.float32)

            @pl.when(slots[i] >= 0)
            def _():
                kept[:, at] = solved[:, pl.ds(pl.multiple_of(slots[i] * BW, BW), BW)]

        width = front.shape[1]
        new = dot_split(split(kept[...]), split(front[0:FW, :])) - front[RHS : RHS + 8, :]
        solved[:, 0:width] = new
        for i in range(NB):
            at = slice(i * BW, i * BW + BW)

            @pl.when(slots[i] >= 0)
            def _():
                solved[:, at] = kept[:, at]

    out[...] = solved[:, 0:FW]


SCALARS = pl.BlockSpec(memory_space=pltpu.SMEM)
WHOLE = pl.BlockSpec(memory_space=pltpu.VMEM)
PARAMS = pltpu.CompilerParams(vmem_limit_bytes=VMEM_LIMIT)


def f32(*shape):
    return jax.ShapeDtypeStruct(shape, jnp.float32)


def scratch(width):
    return [pltpu.VMEM((BW, BW), jnp.float32), pltpu.VMEM((BW, width), jnp.float32), pltpu.SMEM((8,), jnp.int32)]


def leaf_front(devices, tree, maps, leaf, source, observe, perm):
    return pl.pallas_call(
        functools.partial(leaf_kernel, devices),
        out_shape=(f32(SHARED, FW), f32(PACK, BW)),
        in_specs=[SCALARS, SCALARS] + [WHOLE] * 4,
        out_specs=(WHOLE, WHOLE),
        scratch_shapes=scratch(FW),
        compiler_params=PARAMS,
        name="leaf_front",
    )(tree, maps, leaf, source, observe, perm)


def merge(devices, level, tree, maps, own, theirs):
    last = devices >> (level + 1) == 1
    out = (f32(ROWS, COLS),) + (() if last else (f32(PACK, BW),))
    result = pl.pallas_call(
        functools.partial(merge_kernel, devices, level),
        out_shape=out,
        in_specs=[SCALARS, SCALARS, WHOLE, WHOLE],
        out_specs=(WHOLE,) * len(out),
        scratch_shapes=scratch(COLS) + [pltpu.SMEM((8,), jnp.int32)],
        compiler_params=PARAMS,
        name=f"merge_{level}",
    )(tree, maps, own, theirs)
    return result if not last else (result[0], None)


def recover(devices, tree, maps, fronts):
    return pl.pallas_call(
        functools.partial(recover_kernel, devices, len(fronts) - 1),
        out_shape=f32(8, FW),
        in_specs=[SCALARS, SCALARS] + [WHOLE] * len(fronts),
        out_specs=WHOLE,
        scratch_shapes=[pltpu.VMEM((8, FW), jnp.float32), pltpu.VMEM((8, COLS), jnp.float32)],
        compiler_params=PARAMS,
        name="recover",
    )(tree, maps, *fronts)


def partner(block, axis, bit):
    count = lax.axis_size(axis)
    return lax.ppermute(block, axis, [(k, k ^ (1 << bit)) for k in range(count)])


def shards(leaf_matrix, leaf_source, observe, zone_ids, log_perm, block_map):
    leaf_count = lax.axis_size("leaf")
    sub_count = lax.axis_size("sub")
    devices = leaf_count * sub_count
    leaf_bits = leaf_count.bit_length() - 1
    levels = devices.bit_length() - 1
    tree = (lax.axis_index("leaf") + leaf_count * lax.axis_index("sub")).astype(jnp.int32)[None]
    maps = block_map.reshape(-1)
    all_zones = lax.all_gather(log_perm, ("leaf", "sub"), axis=0, tiled=True)
    cells = zone_ids[0]
    perm = jnp.exp(all_zones[cells])
    front, pack = leaf_front(devices, tree, maps, leaf_matrix[0], leaf_source, observe, perm[None])
    fronts = [front]
    for level in range(levels):
        axis, bit = ("leaf", level) if level < leaf_bits else ("sub", level - leaf_bits)
        front, pack = merge(devices, level, tree, maps, front, partner(pack, axis, bit))
        fronts.append(front)
    solution = recover(devices, tree, maps, fronts)
    terms = -perm * solution[0] * solution[1]
    partial = jax.ops.segment_sum(terms, cells, num_segments=all_zones.shape[0])
    gradient = lax.psum_scatter(partial, ("leaf", "sub"), scatter_dimension=0, tiled=True)
    return solution[0][None, :], gradient


def solution(mesh):
    split_all = ("leaf", "sub")
    in_specs = (P(split_all, None, None), P(split_all, None), P(split_all, None), P(split_all, None), P(split_all), P())
    out_specs = (P(split_all, None), P(split_all))
    return jax.shard_map(shards, mesh=mesh, in_specs=in_specs, out_specs=out_specs, check_vma=False)
```

time: 1590 us -> 476 us (0.30); the launches traced: 1570 us -> 474 us
  other arithmetic: 816 us -> 4.68 us
  matrix products: 296 us -> 0 us
  local copies, waits for them, and re-layouts: 172 us -> 6.69 us
  Pallas kernels: 0 us -> 123 us
  waiting for transfers between devices: 184 us -> 226 us
  starting transfers between devices: 18 us -> 47.9 us
  between operations: 32.8 us -> 14.5 us
    another operation x110 -> x0, other arithmetic: 801 us -> none  [the longest x76 451 us: factor_front(): jnp.linalg.cholesky(parent_node[:elimination_count, :elimination_count])]
    another operation x153 -> x0, matrix products: 161 us -> none  [the longest x119 110 us: lower_triangle_solve(): lax.linalg.triangular_solve(front_factor, rhs, left_side=True, lower=True...]
    dot_general x70 -> x0, matrix products: 136 us -> none  [the longest x14 63.2 us: extend_add(): jnp.einsum('pajb,qj->paqb', blocked, chooser, precision=EXACT_ARITHMETIC)]
    pallas_call x0 -> x9, Pallas kernels: none -> 123 us  [the longest x7 116 us: merge(): pl.pallas_call(functools.partial(merge_kernel, devices, level), out_shape...]
    another operation x109 -> x0, local copies, waits for them, and re-layouts: 99.4 us -> none  [the longest x72 75.2 us: lower_triangle_solve(): lax.linalg.triangular_solve(front_factor, rhs, left_side=True, lower=True...]
    ppermute x14 -> x7, waiting for transfers between devices: 38.9 us -> 83.8 us  [partner(): return lax.ppermute(block, axis, [(k, k ^ 1 << bit) for k in range(count)])]
    unnamed x255 -> x18, local copies, waits for them, and re-layouts: 42.5 us -> 3.42 us
    ppermute x14 -> x7, starting transfers between devices: 18 us -> 47.8 us  [partner(): return lax.ppermute(block, axis, [(k, k ^ 1 << bit) for k in range(count)])]
  transfers between devices with their start and end apart: 15 -> 8, of which waited for: 7 -> 8; matrix products, arithmetic and copies ran while one was open for 6% -> 0% of each run, Pallas kernels for 0% -> 0%
where the time goes in v1:
time: 476 us; the launch traced here: 474 us
  waiting for transfers between devices  226 us (47%)
  Pallas kernels  123 us (26%)
  blocking collectives  51.5 us (11%)
  starting transfers between devices  47.9 us (10%)
  between operations  14.5 us (3%)
  local copies, waits for them, and re-layouts  6.69 us (1%)
    unnamed x2, waiting for transfers between devices  142 us
    pallas_call x7, Pallas kernels, merge(): pl.pallas_call(functools.partial(merge_kernel, devices, level), out_shape...  116 us
    ppermute x7, waiting for transfers between devices, partner(): return lax.ppermute(block, axis, [(k, k ^ 1 << bit) for k in range(count)])  83.8 us
    all_gather x1, blocking collectives, shards(): all_zones = lax.all_gather(log_perm, ('leaf', 'sub'), axis=0, tiled=True)  51.5 us
    ppermute x7, starting transfers between devices, partner(): return lax.ppermute(block, axis, [(k, k ^ 1 << bit) for k in range(count)])  47.8 us
  transfers between devices with their start and end apart: 8, of which 8 were waited for; matrix products, arithmetic and copies ran while one was open for 0% of the time, Pallas kernels for 0%

profile of v1, /device:TPU:1, one launch (start us, length us, event | category | flops | bytes accessed | tf_op | source)
XLA Modules:
  0.0 473.9 jit_solution(11024016802888139978)
XLA Ops:
  7.2 0.0 copy-start.4
  7.2 0.0 copy-start.5
  7.2 0.0 copy-start.6
  7.2 0.0 all-reduce.3.cloned.1.call-start
  7.2 0.9 copy.9
  8.1 0.1 reshape.43.map_ref
  8.3 51.5 %all-gather = f32[128,1,128]{2,1,0:T(1,128)S(1)} all-gather(f32[1,1,128]{2,1,0:T(1,128)} %bitcast.18), channel_id=1, replica_groups=mesh['leaf'=8,'sub'=16] {'leaf','sub'}, dimensions={0}, use_global_device_ids=true | all-gather | bytes 66048 | tf_op jit(solution)/shard_map/all_gather | solution.py:291
  59.7 0.7 compare_select_fusion
  60.4 3.1 gather_fusion
  63.6 0.0 copy-done.4
  63.6 0.0 copy-done.5
  63.6 0.0 copy-done.6
  63.6 0.8 leaf_front.1
  64.4 12.3 %collective-permute-start = (f32[1312,128]{1,0:T(8,128)S(1)}, f32[1312,128]{1,0:T(8,128)S(1)}, u32[]{:S(2)}, u32[]{:S(2)}) collective-permute-start(f32[1312,128]{1,0:T(8,128)S(1)} %get-tuple-element.17), channel_id=1, source_target_pairs={{0,16},{16,0},{32,48},{48,32},{64,80},{80,64},{96,112},{112,96},{1... | collective-permute-start | bytes 2015240 | tf_op jit(solution)/shard_map/ppermute | solution.py:280
  76.7 1.7 collective-permute-done.theirs
  78.5 21.1 %merge_0.1 = (f32[648,640]{1,0:T(8,128)S(1)}, f32[1312,128]{1,0:T(8,128)S(1)}) custom-call(s32[1]{0:T(128)} %bitcast.tree_ref, s32[1016]{0:T(1024)S(1)} %reshape.43.map_ref, f32[520,512]{1,0:T(8,128)S(1)} %get-tuple-element.16.own.refs_0_, f32[1312,128]{1,0:T(8,128)S(1)} %collective-permute-done.theirs), custom_call_target="tpu_custom_call" | custom-call | tf_op jit(solution)/shard_map/merge_0/pallas_call | solution.py:254
  99.6 0.1 collective-permute-start.1
  99.7 15.8 %collective-permute-done.1.theirs = f32[1312,128]{1,0:T(8,128)S(1)} collective-permute-done((f32[1312,128]{1,0:T(8,128)S(1)}, f32[1312,128]{1,0:T(8,128)S(1)}, u32[]{:S(2)}, u32[]{:S(2)}) %collective-permute-start.1) | collective-permute-done | bytes 671776 | tf_op jit(solution)/shard_map/ppermute | solution.py:280
  115.5 14.9 %merge_1.1 = (f32[648,640]{1,0:T(8,128)S(1)}, f32[1312,128]{1,0:T(8,128)S(1)}) custom-call(s32[1]{0:T(128)} %bitcast.tree_ref, s32[1016]{0:T(1024)S(1)} %reshape.43.map_ref, f32[648,640]{1,0:T(8,128)S(1)} %get-tuple-element.18.own.refs_1_, f32[1312,128]{1,0:T(8,128)S(1)} %collective-permute-done.1.theirs), custom_call_target="tpu_custom_call" | custom-call | tf_op jit(solution)/shard_map/merge_1/pallas_call | solution.py:254
  130.4 0.1 collective-permute-start.2
  130.5 16.4 %collective-permute-done.2.theirs = f32[1312,128]{1,0:T(8,128)S(1)} collective-permute-done((f32[1312,128]{1,0:T(8,128)S(1)}, f32[1312,128]{1,0:T(8,128)S(1)}, u32[]{:S(2)}, u32[]{:S(2)}) %collective-permute-start.2) | collective-permute-done | bytes 671776 | tf_op jit(solution)/shard_map/ppermute | solution.py:280
  146.9 14.6 %merge_2.1 = (f32[648,640]{1,0:T(8,128)S(1)}, f32[1312,128]{1,0:T(8,128)S(1)}) custom-call(s32[1]{0:T(128)} %bitcast.tree_ref, s32[1016]{0:T(1024)S(1)} %reshape.43.map_ref, f32[648,640]{1,0:T(8,128)S(1)} %get-tuple-element.20.own.refs_2_, f32[1312,128]{1,0:T(8,128)S(1)} %collective-permute-done.2.theirs), custom_call_target="tpu_custom_call" | custom-call | tf_op jit(solution)/shard_map/merge_2/pallas_call | solution.py:254
  161.5 0.1 collective-permute-start.3
  161.6 14.0 %collective-permute-done.3.theirs = f32[1312,128]{1,0:T(8,128)S(1)} collective-permute-done((f32[1312,128]{1,0:T(8,128)S(1)}, f32[1312,128]{1,0:T(8,128)S(1)}, u32[]{:S(2)}, u32[]{:S(2)}) %collective-permute-start.3) | collective-permute-done | bytes 671776 | tf_op jit(solution)/shard_map/ppermute | solution.py:280
  175.6 15.0 %merge_3.1 = (f32[648,640]{1,0:T(8,128)S(1)}, f32[1312,128]{1,0:T(8,128)S(1)}) custom-call(s32[1]{0:T(128)} %bitcast.tree_ref, s32[1016]{0:T(1024)S(1)} %reshape.43.map_ref, f32[648,640]{1,0:T(8,128)S(1)} %get-tuple-element.22.own.refs_3_, f32[1312,128]{1,0:T(8,128)S(1)} %collective-permute-done.3.theirs), custom_call_target="tpu_custom_call" | custom-call | tf_op jit(solution)/shard_map/merge_3/pallas_call | solution.py:254
  190.6 0.0 copy-start
  190.7 0.1 collective-permute-start.4
  190.8 14.6 %collective-permute-done.4.theirs = f32[1312,128]{1,0:T(8,128)S(1)} collective-permute-done((f32[1312,128]{1,0:T(8,128)S(1)}, f32[1312,128]{1,0:T(8,128)S(1)}, u32[]{:S(2)}, u32[]{:S(2)}) %collective-permute-start.4) | collective-permute-done | bytes 671776 | tf_op jit(solution)/shard_map/ppermute | solution.py:280
  205.3 8.1 %merge_4.1 = (f32[648,640]{1,0:T(8,128)S(1)}, f32[1312,128]{1,0:T(8,128)S(1)}) custom-call(s32[1]{0:T(128)} %bitcast.tree_ref, s32[1016]{0:T(1024)S(1)} %reshape.43.map_ref, f32[648,640]{1,0:T(8,128)S(1)} %get-tuple-element.24.own.refs_4_, f32[1312,128]{1,0:T(8,128)S(1)} %collective-permute-done.4.theirs), custom_call_target="tpu_custom_call" | custom-call | tf_op jit(solution)/shard_map/merge_4/pallas_call | solution.py:254
  213.4 0.0 copy-start.1
  213.4 1.8 collective-permute-start.5
  215.2 10.9 %collective-permute-done.5.theirs = f32[1312,128]{1,0:T(8,128)S(1)} collective-permute-done((f32[1312,128]{1,0:T(8,128)S(1)}, f32[1312,128]{1,0:T(8,128)S(1)}, u32[]{:S(2)}, u32[]{:S(2)}) %collective-permute-start.5) | collective-permute-done | bytes 671776 | tf_op jit(solution)/shard_map/ppermute | solution.py:280
  226.2 8.3 %merge_5.1 = (f32[648,640]{1,0:T(8,128)S(1)}, f32[1312,128]{1,0:T(8,128)S(1)}) custom-call(s32[1]{0:T(128)} %bitcast.tree_ref, s32[1016]{0:T(1024)S(1)} %reshape.43.map_ref, f32[648,640]{1,0:T(8,128)S(1)} %get-tuple-element.26.own.refs_5_, f32[1312,128]{1,0:T(8,128)S(1)} %collective-permute-done.5.theirs), custom_call_target="tpu_custom_call" | custom-call | tf_op jit(solution)/shard_map/merge_5/pallas_call | solution.py:254
  234.5 0.0 copy-done
  234.5 0.0 copy-start.2
  234.5 33.4 %collective-permute-start.6 = (f32[1312,128]{1,0:T(8,128)S(1)}, f32[1312,128]{1,0:T(8,128)S(1)}, u32[]{:S(2)}, u32[]{:S(2)}) collective-permute-start(f32[1312,128]{1,0:T(8,128)S(1)} %get-tuple-element.29), channel_id=1, source_target_pairs={{0,8},{1,9},{2,10},{3,11},{4,12},{5,13},{6,14},{7,15},{8,0},{9,1},... | collective-permute-start | bytes 2015240 | tf_op jit(solution)/shard_map/ppermute | solution.py:280
  267.9 10.3 %collective-permute-done.6.theirs = f32[1312,128]{1,0:T(8,128)S(1)} collective-permute-done((f32[1312,128]{1,0:T(8,128)S(1)}, f32[1312,128]{1,0:T(8,128)S(1)}, u32[]{:S(2)}, u32[]{:S(2)}) %collective-permute-start.6) | collective-permute-done | bytes 671776 | tf_op jit(solution)/shard_map/ppermute | solution.py:280
  278.2 34.1 %merge_6.1.refs_7_ = f32[648,640]{1,0:T(8,128)S(1)} custom-call(s32[1]{0:T(128)} %bitcast.tree_ref, s32[1016]{0:T(1024)S(1)} %reshape.43.map_ref, f32[648,640]{1,0:T(8,128)S(1)} %get-tuple-element.28.own.refs_6_, f32[1312,128]{1,0:T(8,128)S(1)} %collective-permute-done.6.theirs), custom_call_target="tpu_custom_call" | custom-call | tf_op jit(solution)/shard_map/merge_6/pallas_call | solution.py:254
  312.4 0.0 copy-done.1
  312.4 0.0 copy-done.2
  312.4 0.0 copy-start.3
  312.4 1.2 copy-done.3
  313.6 5.8 %recover.1 = f32[8,512]{1,0:T(8,128)S(1)} custom-call(s32[1]{0:T(128)} %bitcast.tree_ref, s32[1016]{0:T(1024)S(1)} %reshape.43.map_ref, f32[520,512]{1,0:T(8,128)S(1)} %get-tuple-element.16.own.refs_0_, f32[648,640]{1,0:T(8,128)S(1)} %get-tuple-element.18.own.refs_1_, f32[648,640]{1,0:T(8,128)S(1)} %get-tuple-element.20.own.refs_2_, ...), custom_call_target="tpu_custom_call" | custom-call | tf_op jit(solution)/shard_map/recover/pallas_call | solution.py:267
  319.5 0.0 copy-start.7
  319.5 4.0 scatter_custom_fusion
  323.5 0.0 all-reduce.3.cloned.1.call-update
  323.5 142.0 %all-reduce.3.cloned.1.call-done = f32[16384]{0:T(1024)} async-done(((f32[16384]{0:T(1024)}), f32[16384]{0:T(1024)}) %all-reduce.3.cloned.1.call-update) | async-done | bytes 65552
  465.6 1.3 dynamic-slice
  (5 shorter events, 0.0 us)
Async XLA Ops:
  7.2 56.5 %copy-start.4 = (f32[1,512,512]{2,1,0:T(8,128)S(1)}, f32[1,512,512]{2,1,0:T(8,128)}, u32[]{:S(2)}) copy-start(f32[1,512,512]{2,1,0:T(8,128)} %param.6) | copy-start | bytes 3145732
  7.2 56.5 %copy-start.5 = (f32[1,512]{1,0:T(1,128)S(1)}, f32[1,512]{1,0:T(1,128)}, u32[]{:S(2)}) copy-start(f32[1,512]{1,0:T(1,128)} %source.1) | copy-start | bytes 6148
  7.2 56.5 %copy-start.6 = (f32[1,512]{1,0:T(1,128)S(1)}, f32[1,512]{1,0:T(1,128)}, u32[]{:S(2)}) copy-start(f32[1,512]{1,0:T(1,128)} %observe.1) | copy-start | bytes 6148
  7.2 458.4 %all-reduce.3.cloned.1.call-start = ((), (), s32[]{:S(2)}) async-start(), calls=%async_computation | async-start | bytes 131072
  64.4 14.0 %collective-permute-start = (f32[1312,128]{1,0:T(8,128)S(1)}, f32[1312,128]{1,0:T(8,128)S(1)}, u32[]{:S(2)}, u32[]{:S(2)}) collective-permute-start(f32[1312,128]{1,0:T(8,128)S(1)} %get-tuple-element.17), channel_id=1, source_target_pairs={{0,16},{16,0},{32,48},{48,32},{64,80},{80,64},{96,112},{112,96},{1... | collective-permute-start | bytes 2015240 | tf_op jit(solution)/shard_map/ppermute | solution.py:280
  99.6 15.9 %collective-permute-start.1 = (f32[1312,128]{1,0:T(8,128)S(1)}, f32[1312,128]{1,0:T(8,128)S(1)}, u32[]{:S(2)}, u32[]{:S(2)}) collective-permute-start(f32[1312,128]{1,0:T(8,128)S(1)} %get-tuple-element.19), channel_id=1, source_target_pairs={{0,32},{16,48},{32,0},{48,16},{64,96},{80,112},{96,64},{112,80},{1... | collective-permute-start | bytes 2015240 | tf_op jit(solution)/shard_map/ppermute | solution.py:280
  130.4 16.5 %collective-permute-start.2 = (f32[1312,128]{1,0:T(8,128)S(1)}, f32[1312,128]{1,0:T(8,128)S(1)}, u32[]{:S(2)}, u32[]{:S(2)}) collective-permute-start(f32[1312,128]{1,0:T(8,128)S(1)} %get-tuple-element.21), channel_id=1, source_target_pairs={{0,64},{16,80},{32,96},{48,112},{64,0},{80,16},{96,32},{112,48},{1... | collective-permute-start | bytes 2015240 | tf_op jit(solution)/shard_map/ppermute | solution.py:280
  161.5 14.1 %collective-permute-start.3 = (f32[1312,128]{1,0:T(8,128)S(1)}, f32[1312,128]{1,0:T(8,128)S(1)}, u32[]{:S(2)}, u32[]{:S(2)}) collective-permute-start(f32[1312,128]{1,0:T(8,128)S(1)} %get-tuple-element.23), channel_id=1, source_target_pairs={{0,1},{1,0},{2,3},{3,2},{4,5},{5,4},{6,7},{7,6},{8,9},{9,8},{10,11... | collective-permute-start | bytes 2015240 | tf_op jit(solution)/shard_map/ppermute | solution.py:280
  190.6 43.8 %copy-start = (f32[648,640]{1,0:T(8,128)}, f32[648,640]{1,0:T(8,128)S(1)}, u32[]{:S(2)}) copy-start(f32[648,640]{1,0:T(8,128)S(1)} %get-tuple-element.24.own.refs_4_) | copy-start | bytes 4976644
  190.7 14.7 %collective-permute-start.4 = (f32[1312,128]{1,0:T(8,128)S(1)}, f32[1312,128]{1,0:T(8,128)S(1)}, u32[]{:S(2)}, u32[]{:S(2)}) collective-permute-start(f32[1312,128]{1,0:T(8,128)S(1)} %get-tuple-element.25), channel_id=1, source_target_pairs={{0,2},{1,3},{2,0},{3,1},{4,6},{5,7},{6,4},{7,5},{8,10},{9,11},{10,... | collective-permute-start | bytes 2015240 | tf_op jit(solution)/shard_map/ppermute | solution.py:280
  213.4 99.0 %copy-start.1 = (f32[648,640]{1,0:T(8,128)}, f32[648,640]{1,0:T(8,128)S(1)}, u32[]{:S(2)}) copy-start(f32[648,640]{1,0:T(8,128)S(1)} %get-tuple-element.26.own.refs_5_) | copy-start | bytes 4976644
  213.4 12.8 %collective-permute-start.5 = (f32[1312,128]{1,0:T(8,128)S(1)}, f32[1312,128]{1,0:T(8,128)S(1)}, u32[]{:S(2)}, u32[]{:S(2)}) collective-permute-start(f32[1312,128]{1,0:T(8,128)S(1)} %get-tuple-element.27), channel_id=1, source_target_pairs={{0,4},{1,5},{2,6},{3,7},{4,0},{5,1},{6,2},{7,3},{8,12},{9,13},{10,... | collective-permute-start | bytes 2015240 | tf_op jit(solution)/shard_map/ppermute | solution.py:280
  234.5 77.9 %copy-start.2 = (f32[648,640]{1,0:T(8,128)}, f32[648,640]{1,0:T(8,128)S(1)}, u32[]{:S(2)}) copy-start(f32[648,640]{1,0:T(8,128)S(1)} %get-tuple-element.28.own.refs_6_) | copy-start | bytes 4976644
  234.5 43.8 %collective-permute-start.6 = (f32[1312,128]{1,0:T(8,128)S(1)}, f32[1312,128]{1,0:T(8,128)S(1)}, u32[]{:S(2)}, u32[]{:S(2)}) collective-permute-start(f32[1312,128]{1,0:T(8,128)S(1)} %get-tuple-element.29), channel_id=1, source_target_pairs={{0,8},{1,9},{2,10},{3,11},{4,12},{5,13},{6,14},{7,15},{8,0},{9,1},... | collective-permute-start | bytes 2015240 | tf_op jit(solution)/shard_map/ppermute | solution.py:280
  312.4 1.3 copy-start.3
  319.5 147.3 %copy-start.7 = (f32[1,512]{1,0:T(1,128)}, f32[1,512]{1,0:T(1,128)S(1)}, u32[]{:S(2)}) copy-start(f32[1,512]{1,0:T(1,128)S(1)} %get-tuple-element.31) | copy-start | bytes 6148
Sparse Core Ops, SparseCore 0:
  323.6 141.8 all-reduce.2
